TPU v7x, 32 devices: a whole 2x2x4 slice. The times are simulated.
32 devices in a mesh: row: 8 (over y, x, core), col: 4 (over z).
Axes of the slice: x: 2, y: 2, z: 4, core: 2. Of those that a mesh axis runs over, the one named last changes fastest.
Arguments:
- noise: float32 [512, 36, 1024], P('col', None, 'row'), may hold values from -6 to 6
- factor: bfloat16 [31, 1024, 3, 5120], P(None, 'row', None, 'col'), may hold values from -0.0390625 to 0.0390625
- dinv: bfloat16 [3, 5120, 5, 1024], P(None, 'col', None, 'row'), as said below
Outputs:
- solved: bfloat16 [3, 5120, 512], P(None, 'col')
- remaining: float32 [512, 36, 1024], P('col', None, 'row')
Inputs may be any that keep to these rules, and one draw needn't show every extreme that they name: dinv[s], read as a 5120 x 5120 matrix, is lower triangular with a positive diagonal.
All inputs are finite; a program needn't handle non-finite values.
Results may differ from a plain program's by a relative error of at most 0.007.
Values may be sent and summed in bfloat16 or wider, within the bound.
A program may use at most 128 MiB of HBM per device.

v0:
```python
import jax
import jax.numpy as jnp
from jax import lax
from jax.sharding import PartitionSpec as P


def local(noise, factor, dinv):
    step_count = dinv.shape[0]
    rounds = dinv.shape[2]
    work = noise
    solved_list = []
    for step_idx in range(step_count):
        current = work[:, step_idx * rounds : (step_idx + 1) * rounds, :].astype(jnp.bfloat16)
        gathered = lax.all_gather(current, "col", axis=0, tiled=True).astype(jnp.float32)
        inverse = dinv[step_idx].astype(jnp.float32)
        partial_sum = lax.dot_general(inverse, gathered, (((1, 2), (1, 2)), ((), ())))
        solution = lax.psum(partial_sum, "row").astype(jnp.bfloat16)
        solved_list.append(solution)
        solution_wide = solution.astype(jnp.float32)
        panel_rows = factor[step_idx * rounds :, :, step_idx, :].astype(jnp.float32)
        reduced = lax.psum_scatter(
            lax.dot_general(solution_wide, panel_rows, (((0,), (2,)), ((), ()))),
            "col",
            scatter_dimension=0,
            tiled=True,
        )
        work = work.at[:, (step_idx + 1) * rounds :, :].add(-reduced)
    return (jnp.stack(solved_list), work)


def solution(mesh):
    placed = (P("col", None, "row"), P(None, "row", None, "col"), P(None, "col", None, "row"))
    return jax.shard_map(
        local,
        mesh=mesh,
        in_specs=placed,
        out_specs=(P(None, "col", None), P("col", None, "row")),
        check_vma=False,
    )
```

profile of v0, /device:TPU:0, one launch (start us, length us, event | category | flops | bytes accessed | tf_op | source)
XLA Modules:
  0.0 658.9 jit_solution(497371121084972622)
XLA Ops:
  7.2 0.0 reduce-scatter.4.cloned.1.call-start
  7.2 0.0 copy-start.3
  7.2 1.8 copy.36
  9.1 19.8 %all_gather.9 = bf16[512,5,128]{2,0,1:T(8,128)(2,1)S(1)} all-gather(bf16[128,5,128]{2,0,1:T(8,128)(2,1)S(1)} %slice.157), channel_id=1, replica_groups=mesh['row'=8,'col'=4] {'col'}, dimensions={0}, use_global_device_ids=true | all-gather | bytes 819200 | tf_op jit(solution)/shard_map/all_gather | solution.py:14
  28.8 2.7 convolution_bitcast_fusion.2
  31.5 60.5 %all-reduce.3 = bf16[1280,512]{1,0:T(8,128)(2,1)} all-reduce(f32[1280,512]{1,0:T(8,128)} %convolution_bitcast_fusion.2), channel_id=1, replica_groups=mesh['row'=8,'col'=4] {'row'}, use_global_device_ids=true, to_apply=%region_0.0 | all-reduce | flops 655360 | bytes 3932160 | tf_op jit(solution)/shard_map/psum | solution.py:17
  92.0 10.6 %fusion = f32[512,31,128]{2,0,1:T(8,128)} fusion(bf16[31,128,3,1280]{3,1,2,0:T(8,128)(2,1)} %param.10, bf16[1280,512]{1,0:T(8,128)(2,1)} %all-reduce.3), kind=kOutput, calls=%fused_computation | convolution fusion | flops 5200936960 | bytes 19595264 | tf_op jit(solution)/shard_map/dot_general | solution.py:22
  102.6 0.0 reduce-scatter.4.cloned.1.call-update
  102.7 0.0 reduce-scatter.6.cloned.1.call-start
  102.7 140.1 %reduce-scatter.4.cloned.1.call-done = f32[128,31,128]{2,0,1:T(8,128)} async-done(((f32[512,31,128]{2,0,1:T(8,128)}), f32[128,31,128]{2,0,1:T(8,128)}) %reduce-scatter.4.cloned.1.call-update) | async-done | bytes 2031632 | tf_op jit(solution)/shard_map/reduce_scatter | solution.py:21
  242.8 2.4 constant_dynamic-update-slice_fusion.1
  245.2 1.3 copy-done.1
  246.5 17.5 %all_gather.10 = bf16[512,5,128]{2,0,1:T(8,128)(2,1)S(1)} all-gather(bf16[128,5,128]{2,0,1:T(8,128)(2,1)S(1)} %slice.156), channel_id=1, replica_groups=mesh['row'=8,'col'=4] {'col'}, dimensions={0}, use_global_device_ids=true | all-gather | bytes 819200 | tf_op jit(solution)/shard_map/all_gather | solution.py:14
  264.0 4.1 convolution_bitcast_fusion.1
  268.2 61.0 %all-reduce.4 = bf16[1280,512]{1,0:T(8,128)(2,1)} all-reduce(f32[1280,512]{1,0:T(8,128)} %convolution_bitcast_fusion.1), channel_id=1, replica_groups=mesh['row'=8,'col'=4] {'row'}, use_global_device_ids=true, to_apply=%region_2.0 | all-reduce | flops 655360 | bytes 3932160 | tf_op jit(solution)/shard_map/psum | solution.py:17
  329.2 9.5 %fusion.3 = f32[512,26,128]{2,0,1:T(8,128)} fusion(bf16[31,128,3,1280]{3,1,2,0:T(8,128)(2,1)} %param.10, bf16[1280,512]{1,0:T(8,128)(2,1)} %all-reduce.4), kind=kOutput, calls=%fused_computation.3 | convolution fusion | flops 4362076160 | bytes 16646144 | tf_op jit(solution)/shard_map/dot_general | solution.py:22
  338.7 0.0 reduce-scatter.6.cloned.1.call-update
  338.7 0.0 reduce-scatter.8.cloned.1.call-start
  338.8 118.4 %reduce-scatter.6.cloned.1.call-done = f32[128,26,128]{2,0,1:T(8,128)} async-done(((f32[512,26,128]{2,0,1:T(8,128)}), f32[128,26,128]{2,0,1:T(8,128)}) %reduce-scatter.6.cloned.1.call-update) | async-done | bytes 1703952 | tf_op jit(solution)/shard_map/reduce_scatter | solution.py:21
  457.2 2.3 constant_dynamic-update-slice_fusion
  459.5 0.0 copy-start.2
  459.5 1.2 copy-done.2
  460.7 17.4 %all_gather.11 = bf16[512,5,128]{2,0,1:T(8,128)(2,1)S(1)} all-gather(bf16[128,5,128]{2,0,1:T(8,128)(2,1)S(1)} %slice.155), channel_id=1, replica_groups=mesh['row'=8,'col'=4] {'col'}, dimensions={0}, use_global_device_ids=true | all-gather | bytes 819200 | tf_op jit(solution)/shard_map/all_gather | solution.py:14
  478.1 4.1 convolution_bitcast_fusion
  482.2 60.9 %all-reduce.5 = bf16[1280,512]{1,0:T(8,128)(2,1)} all-reduce(f32[1280,512]{1,0:T(8,128)} %convolution_bitcast_fusion), channel_id=1, replica_groups=mesh['row'=8,'col'=4] {'row'}, use_global_device_ids=true, to_apply=%region_4.0 | all-reduce | flops 655360 | bytes 3932160 | tf_op jit(solution)/shard_map/psum | solution.py:17
  543.2 8.4 %fusion.6 = f32[512,21,128]{2,0,1:T(8,128)} fusion(bf16[31,128,3,1280]{3,1,2,0:T(8,128)(2,1)} %param.10, bf16[1280,512]{1,0:T(8,128)(2,1)} %all-reduce.5), kind=kOutput, calls=%fused_computation.6 | convolution fusion | flops 3523215360 | bytes 13697024 | tf_op jit(solution)/shard_map/dot_general | solution.py:22
  551.6 0.0 reduce-scatter.8.cloned.1.call-update
  551.6 3.6 pad_maximum_fusion
  555.2 93.7 %reduce-scatter.8.cloned.1.call-done = f32[128,21,128]{2,0,1:T(8,128)} async-done(((f32[512,21,128]{2,0,1:T(8,128)}), f32[128,21,128]{2,0,1:T(8,128)}) %reduce-scatter.8.cloned.1.call-update) | async-done | bytes 1376272 | tf_op jit(solution)/shard_map/reduce_scatter | solution.py:21
  649.0 1.9 fusion.15
  650.9 0.0 copy-start
  650.9 1.4 copy-done
  (5 shorter events, 0.1 us)
Async XLA Ops:
  7.2 235.7 %reduce-scatter.4.cloned.1.call-start = ((), (), s32[]{:S(2)}) async-start(), calls=%async_computation.3 | async-start | bytes 10158080 | tf_op jit(solution)/shard_map/reduce_scatter | solution.py:21
  7.2 21.6 %copy-start.3 = (bf16[3,1280,5,128]{3,1,2,0:T(8,128)(2,1)S(1)}, bf16[3,1280,5,128]{3,1,2,0:T(8,128)(2,1)}, u32[]{:S(2)}) copy-start(bf16[3,1280,5,128]{3,1,2,0:T(8,128)(2,1)} %param.11) | copy-start | bytes 14745604
  102.7 354.5 %reduce-scatter.6.cloned.1.call-start = ((), (), s32[]{:S(2)}) async-start(), calls=%async_computation.4 | async-start | bytes 8519680 | tf_op jit(solution)/shard_map/reduce_scatter | solution.py:21
  245.2 1.3 copy-start.1
  338.7 310.2 %reduce-scatter.8.cloned.1.call-start = ((), (), s32[]{:S(2)}) async-start(), calls=%async_computation.5 | async-start | bytes 6881280 | tf_op jit(solution)/shard_map/reduce_scatter | solution.py:21
  459.5 1.2 copy-start.2
  650.9 1.4 copy-start
Sparse Core Ops, SparseCore 0:
  102.8 139.9 reduce-scatter.3
  338.8 118.3 reduce-scatter.5
  551.7 97.1 reduce-scatter.7
where the time goes:
time: 659 us
  waiting for transfers between devices  352 us (53%)
  blocking collectives  237 us (36%)
  matrix products  39.6 us (6%)
  between operations  13.8 us (2%)
  other arithmetic  10.2 us (2%)
    reduce_scatter x3, waiting for transfers between devices, local(): lax.psum_scatter(lax.dot_general(solution_wide, panel_rows, (((0,), (2,))...  352 us
    psum x3, blocking collectives, local(): solution = lax.psum(partial_sum, 'row').astype(jnp.bfloat16)  182 us
    all_gather x3, blocking collectives, local(): lax.all_gather(current, 'col', axis=0, tiled=True).astype(jnp.float32)  54.6 us
    dot_general x3, matrix products, local(): lax.dot_general(solution_wide, panel_rows, (((0,), (2,)), ((), ())))  28.6 us
  transfers between devices with their start and end apart: 3, of which 3 were waited for; matrix products, arithmetic and copies ran while one was open for 1% of the time, Pallas kernels for 0%

commit v1 on v0

v1 whole, which is shorter than its diff:
```python
import jax
import jax.numpy as jnp
from jax import lax
from jax.sharding import PartitionSpec as P

BF16 = jnp.bfloat16
F32 = jnp.float32


def local(noise, factor, dinv):
    steps = dinv.shape[0]
    rounds = dinv.shape[2]
    work = jnp.transpose(noise, (1, 0, 2))
    rows = jnp.transpose(factor, (2, 0, 1, 3))
    blocks = jnp.transpose(dinv, (0, 2, 1, 3))
    solved = []
    done = []
    for s in range(steps):
        current = work[s * rounds : (s + 1) * rounds]
        if s > 0:
            update = sum(
                jnp.einsum("apq,qh->ahp", rows[t, (s - 1) * rounds : s * rounds], solved[t], preferred_element_type=F32)
                for t in range(s)
            )
            current = current - lax.psum_scatter(update.astype(BF16), "col", scatter_dimension=1, tiled=True).astype(F32)
        done.append(current)
        gathered = lax.all_gather(current.astype(BF16), "col", axis=1, tiled=True)
        partial_sum = jnp.einsum("dqp,dhp->qh", blocks[s], gathered, preferred_element_type=F32)
        solved.append(lax.psum(partial_sum.astype(BF16), "row"))
    update = sum(
        jnp.einsum("apq,qh->ahp", rows[t, (steps - 1) * rounds :], solved[t], preferred_element_type=F32)
        for t in range(steps)
    )
    last = work[steps * rounds :] - lax.psum_scatter(update.astype(BF16), "col", scatter_dimension=1, tiled=True).astype(F32)
    done.append(last)
    remaining = jnp.transpose(jnp.concatenate(done, axis=0), (1, 0, 2))
    return jnp.stack(solved), remaining


def solution(mesh):
    placed = (P("col", None, "row"), P(None, "row", None, "col"), P(None, "col", None, "row"))
    return jax.shard_map(
        local,
        mesh=mesh,
        in_specs=placed,
        out_specs=(P(None, "col", None), P("col", None, "row")),
        check_vma=False,
    )
```

time: 659 us -> 380 us (0.58)
  blocking collectives: 237 us -> 53.1 us
  waiting for transfers between devices: 352 us -> 236 us
  local copies, waits for them, and re-layouts: 5.76 us -> 22.5 us
    reduce_scatter x3, waiting for transfers between devices: 352 us -> 92.8 us  [local(): lax.psum_scatter(update.astype(BF16), 'col', scatter_dimension=1, tiled=T...]
    psum x3 -> x0, blocking collectives: 182 us -> none  [local(): solution = lax.psum(partial_sum, 'row').astype(jnp.bfloat16)]
    psum x0 -> x3, waiting for transfers between devices: none -> 143 us  [local(): solved.append(lax.psum(partial_sum.astype(BF16), 'row'))]
    unnamed x9, local copies, waits for them, and re-layouts: 5.69 us -> 21.5 us
    scatter-add x3 -> x0, other arithmetic: 6.61 us -> none  [local(): work = work.at[:, (step_idx + 1) * rounds:, :].add(-reduced)]
    dot_general x6 -> x9, matrix products: 39.6 us -> 44.9 us  [the longest x3 23.1 us: local(): jnp.einsum('apq,qh->ahp', rows[t, (steps - 1) * rounds:], solved[t], pref...]
  transfers between devices with their start and end apart: 3 -> 6, of which waited for: 3 -> 6; matrix products, arithmetic and copies ran while one was open for 1% -> 9% of each run, Pallas kernels for 0% -> 0%
where the time goes in v1:
time: 380 us; the launch traced here: 379 us
  waiting for transfers between devices  236 us (62%)
  blocking collectives  53.1 us (14%)
  matrix products  44.9 us (12%)
  local copies, waits for them, and re-layouts  22.5 us (6%)
  between operations  14.2 us (4%)
  other arithmetic  8.37 us (2%)
    psum x3, waiting for transfers between devices, local(): solved.append(lax.psum(partial_sum.astype(BF16), 'row'))  143 us
    reduce_scatter x3, waiting for transfers between devices, local(): lax.psum_scatter(update.astype(BF16), 'col', scatter_dimension=1, tiled=T...  92.8 us
    all_gather x3, blocking collectives, local(): gathered = lax.all_gather(current.astype(BF16), 'col', axis=1, tiled=True)  53.1 us
    dot_general x3, matrix products, local(): jnp.einsum('apq,qh->ahp', rows[t, (steps - 1) * rounds:], solved[t], pref...  23.1 us
    unnamed x9, local copies, waits for them, and re-layouts  21.5 us
    dot_general x3, matrix products, local(): jnp.einsum('dqp,dhp->qh', blocks[s], gathered, preferred_element_type=F32)  11.1 us
    dot_general x3, matrix products, local(): jnp.einsum('apq,qh->ahp', rows[t, (s - 1) * rounds:s * rounds], solved[t]...  10.7 us
  transfers between devices with their start and end apart: 6, of which 6 were waited for; matrix products, arithmetic and copies ran while one was open for 9% of the time, Pallas kernels for 0%

profile of v1, /device:TPU:0, one launch (start us, length us, event | category | flops | bytes accessed | tf_op | source)
XLA Modules:
  0.0 379.1 jit_solution(9028364072961737539)
XLA Ops:
  7.2 0.0 all-reduce.4.cloned.1.call-start
  7.2 1.0 slice.99
  8.2 19.6 %all_gather.9 = bf16[5,512,128]{2,1,0:T(8,128)(2,1)S(1)} all-gather(bf16[5,128,128]{2,1,0:T(8,128)(2,1)S(1)} %slice.99), channel_id=1, replica_groups=mesh['row'=8,'col'=4] {'col'}, dimensions={1}, use_global_device_ids=true | all-gather | bytes 819200 | tf_op jit(solution)/shard_map/all_gather | solution.py:27
  27.8 3.7 fusion.3
  31.5 0.0 all-reduce.4.cloned.1.call-update
  31.6 0.0 reduce-scatter.4.cloned.1.call-start
  31.6 21.5 %copy.31 = bf16[31,128,3,1280]{3,1,0,2:T(8,128)(2,1)} copy(bf16[31,128,3,1280]{3,1,2,0:T(8,128)(2,1)} %param.4) | data formatting | bytes 60948480 | tf_op args[1]
  53.1 36.7 %all-reduce.4.cloned.1.call-done = bf16[1280,512]{1,0:T(8,128)(2,1)} async-done(((bf16[1280,512]{1,0:T(8,128)(2,1)}), bf16[1280,512]{1,0:T(8,128)(2,1)}) %all-reduce.4.cloned.1.call-update) | async-done | bytes 1310736 | tf_op jit(solution)/shard_map/psum | solution.py:29
  89.7 4.0 %fusion.24 = bf16[5,512,128]{2,1,0:T(8,128)(2,1)} fusion(bf16[3,31,128,1280]{3,2,1,0:T(8,128)(2,1)} %bitcast.100, bf16[1280,512]{1,0:T(8,128)(2,1)} %all-reduce.4.cloned.1.call-done), kind=kOutput, calls=%fused_computation.39 | convolution fusion | flops 839188480 | bytes 3604480 | tf_op jit(solution)/shard_map/apq,qh->ahp/dot_general | solution.py:22
  93.8 0.0 all-reduce.6.cloned.1.call-start
  93.9 21.5 %reduce-scatter.4.cloned.1.call-done = bf16[5,128,128]{2,1,0:T(8,128)(2,1)} async-done(((bf16[5,512,128]{2,1,0:T(8,128)(2,1)}), bf16[5,128,128]{2,1,0:T(8,128)(2,1)}) %reduce-scatter.4.cloned.1.call-update) | async-done | bytes 163856 | tf_op jit(solution)/shard_map/reduce_scatter | solution.py:25
  115.3 1.0 fusion.28
  116.3 16.7 %all_gather.10 = bf16[5,512,128]{2,1,0:T(8,128)(2,1)S(1)} all-gather(bf16[5,128,128]{2,1,0:T(8,128)(2,1)S(1)} %get-tuple-element.4), channel_id=1, replica_groups=mesh['row'=8,'col'=4] {'col'}, dimensions={1}, use_global_device_ids=true | all-gather | bytes 819200 | tf_op jit(solution)/shard_map/all_gather | solution.py:27
  133.0 3.7 fusion.8
  136.8 0.0 reduce-scatter.6.cloned.1.call-start
  136.8 57.3 %all-reduce.6.cloned.1.call-done = bf16[1280,512]{1,0:T(8,128)(2,1)} async-done(((bf16[1280,512]{1,0:T(8,128)(2,1)}), bf16[1280,512]{1,0:T(8,128)(2,1)}) %all-reduce.6.cloned.1.call-update) | async-done | bytes 1310736 | tf_op jit(solution)/shard_map/psum | solution.py:29
  194.1 3.2 fusion.9
  197.3 3.5 fusion.21
  200.8 0.0 all-reduce.8.cloned.1.call-start
  200.9 21.5 %reduce-scatter.6.cloned.1.call-done = bf16[5,128,128]{2,1,0:T(8,128)(2,1)} async-done(((bf16[5,512,128]{2,1,0:T(8,128)(2,1)}), bf16[5,128,128]{2,1,0:T(8,128)(2,1)}) %reduce-scatter.6.cloned.1.call-update) | async-done | bytes 163856 | tf_op jit(solution)/shard_map/reduce_scatter | solution.py:25
  222.4 1.0 fusion.27
  223.4 16.7 %all_gather.11 = bf16[5,512,128]{2,1,0:T(8,128)(2,1)S(1)} all-gather(bf16[5,128,128]{2,1,0:T(8,128)(2,1)S(1)} %get-tuple-element.2), channel_id=1, replica_groups=mesh['row'=8,'col'=4] {'col'}, dimensions={1}, use_global_device_ids=true | all-gather | bytes 819200 | tf_op jit(solution)/shard_map/all_gather | solution.py:27
  240.1 3.7 fusion.7
  243.8 0.2 reduce-scatter.8.cloned.1.call-start
  244.1 8.4 %fusion.1 = f32[512,21,128]{2,0,1:T(8,128)} fusion(bf16[3,31,128,1280]{3,2,1,0:T(8,128)(2,1)} %bitcast.103, bf16[1280,512]{1,0:T(8,128)(2,1)} %all-reduce.6.cloned.1.call-done), kind=kOutput, calls=%fused_computation.4 | convolution fusion | flops 3523215360 | bytes 13697024 | tf_op jit(solution)/shard_map/apq,qh->ahp/dot_general | solution.py:31
  252.4 48.7 %all-reduce.8.cloned.1.call-done = bf16[1280,512]{1,0:T(8,128)(2,1)} async-done(((bf16[1280,512]{1,0:T(8,128)(2,1)}), bf16[1280,512]{1,0:T(8,128)(2,1)}) %all-reduce.8.cloned.1.call-update) | async-done | bytes 1310736 | tf_op jit(solution)/shard_map/psum | solution.py:29
  301.2 6.9 %fusion = f32[512,21,128]{2,0,1:T(8,128)S(1)} fusion(bf16[3,31,128,1280]{3,2,1,0:T(8,128)(2,1)} %bitcast.104, bf16[1280,512]{1,0:T(8,128)(2,1)} %all-reduce.8.cloned.1.call-done), kind=kOutput, calls=%fused_computation.2 | convolution fusion | flops 3523215360 | bytes 13697024 | tf_op jit(solution)/shard_map/apq,qh->ahp/dot_general | solution.py:31
  308.2 7.7 %fusion.6 = bf16[21,512,128]{2,1,0:T(8,128)(2,1)} fusion(f32[512,21,128]{2,0,1:T(8,128)S(1)} %fusion, f32[512,21,128]{2,0,1:T(8,128)S(1)} %copy-done.3, bf16[3,31,128,1280]{3,2,1,0:T(8,128)(2,1)} %bitcast.105, bf16[1280,512]{1,0:T(8,128)(2,1)S(1)} %copy-done.2), kind=kOutput, calls=%fused_computation.15 | convolution fusion | flops 3527344128 | bytes 21954560 | tf_op jit(solution)/shard_map/apq,qh->ahp/dot_general | solution.py:31
  315.9 3.6 pad_maximum_fusion
  319.5 49.9 %reduce-scatter.8.cloned.1.call-done = bf16[21,128,128]{2,1,0:T(8,128)(2,1)} async-done(((bf16[21,512,128]{2,1,0:T(8,128)(2,1)}), bf16[21,128,128]{2,1,0:T(8,128)(2,1)}) %reduce-scatter.8.cloned.1.call-update) | async-done | bytes 688144 | tf_op jit(solution)/shard_map/reduce_scatter | solution.py:34
  369.4 1.2 slice_subtract_fusion
  370.7 1.6 maximum_bitcast_fusion
  (13 shorter events, 0.1 us)
Async XLA Ops:
  7.2 82.6 %all-reduce.4.cloned.1.call-start = ((), (), s32[]{:S(2)}) async-start(), calls=%async_computation.3 | async-start | bytes 2621440 | tf_op jit(solution)/shard_map/psum | solution.py:29
  31.6 83.8 %reduce-scatter.4.cloned.1.call-start = ((), (), s32[]{:S(2)}) async-start(), calls=%async_computation.4 | async-start | bytes 819200 | tf_op jit(solution)/shard_map/reduce_scatter | solution.py:25
  89.7 25.6 %copy-start = (f32[128,36,128]{2,0,1:T(8,128)S(1)}, f32[128,36,128]{2,0,1:T(8,128)}, u32[]{:S(2)}) copy-start(f32[128,36,128]{2,0,1:T(8,128)} %param.3) | copy-start | bytes 7077892
  93.8 100.3 %all-reduce.6.cloned.1.call-start = ((), (), s32[]{:S(2)}) async-start(), calls=%async_computation.5 | async-start | bytes 2621440 | tf_op jit(solution)/shard_map/psum | solution.py:29
  136.8 85.6 %reduce-scatter.6.cloned.1.call-start = ((), (), s32[]{:S(2)}) async-start(), calls=%async_computation.6 | async-start | bytes 819200 | tf_op jit(solution)/shard_map/reduce_scatter | solution.py:25
  194.1 3.2 copy-start.1
  200.8 100.3 %all-reduce.8.cloned.1.call-start = ((), (), s32[]{:S(2)}) async-start(), calls=%async_computation.7 | async-start | bytes 2621440 | tf_op jit(solution)/shard_map/psum | solution.py:29
  243.8 125.6 %reduce-scatter.8.cloned.1.call-start = ((), (), s32[]{:S(2)}) async-start(), calls=%async_computation.8 | async-start | bytes 3440640 | tf_op jit(solution)/shard_map/reduce_scatter | solution.py:34
  301.2 7.0 %copy-start.2 = (bf16[1280,512]{1,0:T(8,128)(2,1)S(1)}, bf16[1280,512]{1,0:T(8,128)(2,1)}, u32[]{:S(2)}) copy-start(bf16[1280,512]{1,0:T(8,128)(2,1)} %all-reduce.4.cloned.1.call-done) | copy-start | bytes 3932164
  301.2 7.0 %copy-start.3 = (f32[512,21,128]{2,0,1:T(8,128)S(1)}, f32[512,21,128]{2,0,1:T(8,128)}, u32[]{:S(2)}) copy-start(f32[512,21,128]{2,0,1:T(8,128)} %fusion.1) | copy-start | bytes 16515076
Sparse Core Ops, SparseCore 0:
  31.7 58.0 all-reduce.3
  93.9 21.3 reduce-scatter.3
  136.9 57.2 all-reduce.5
  201.0 21.3 reduce-scatter.5
  244.0 57.1 all-reduce.7
  316.0 53.3 reduce-scatter.7

commit v2 on v0

v2 whole, which is shorter than its diff:
```python
import functools

import jax
import jax.numpy as jnp
from jax import lax
from jax.experimental import pallas as pl
from jax.experimental.pallas import tpu as pltpu
from jax.sharding import PartitionSpec as P

BF16 = jnp.bfloat16
F32 = jnp.float32
CHAINS = 2
SLOTS = 3
QB = 256


def dot_t(a, b):
    return lax.dot_general(a, b, (((1,), (1,)), ((), ())), preferred_element_type=F32)


def remote(src, dst, send_sem, recv_sem, axis, index):
    return pltpu.make_async_remote_copy(
        src_ref=src,
        dst_ref=dst,
        send_sem=send_sem,
        recv_sem=recv_sem,
        device_id={axis: index},
        device_id_type=pl.DeviceIdType.MESH,
    )


def kernel(
    nr, nc, noise, factor, dinv, out_solved, out_rest,
    dv, lp, lf, st, cur, wsum, rsend, rrecv, pz, zsend, zrecv, pf, frecv,
    dv_sem, lp_sem, lf_sem, out_sem,
    g_ss, g_rs, r_ss, r_rs, z_ss, z_rs, f_ss, f_rs,
):
    steps, rounds, width = dv.shape[0], dv.shape[1], dv.shape[2]
    hl = noise.shape[1]
    hc = hl // CHAINS
    rows = nc * hc
    groups, gs = pf.shape[0], lf.shape[2]
    bits = nr.bit_length() - 1
    first = (steps - 1) * rounds
    r = lax.axis_index("row")
    c = lax.axis_index("col")
    right = jnp.minimum(c + 1, nc - 1)
    left = jnp.maximum(c - 1, 0)
    has_left = c > 0
    has_right = c < nc - 1

    def partner(b):
        return r + (1 - 2 * ((r // (1 << b)) % 2)) * (1 << b)

    dv_copy = [pltpu.make_async_copy(dinv.at[s], dv.at[s], dv_sem.at[s]) for s in range(steps)]
    pairs = [(s, t) for s in range(1, steps) for t in range(s)]
    lp_copy = [
        pltpu.make_async_copy(factor.at[pl.ds((s - 1) * rounds, rounds), t], lp.at[i], lp_sem.at[i])
        for i, (s, t) in enumerate(pairs)
    ]

    def lf_copy(group, t):
        slot = lax.rem(group, SLOTS)
        return pltpu.make_async_copy(
            factor.at[pl.ds(first + group * gs, gs), t], lf.at[slot, t], lf_sem.at[slot, t]
        )

    for copy in dv_copy + lp_copy:
        copy.start()
    for group in range(min(SLOTS, groups)):
        for t in range(steps):
            lf_copy(group, t).start()

    barrier = pltpu.get_barrier_semaphore()
    for b in range(bits):
        pl.semaphore_signal(
            barrier, inc=1, device_id={"row": partner(b)}, device_id_type=pl.DeviceIdType.MESH
        )

    @pl.when(has_left)
    def _():
        pl.semaphore_signal(barrier, inc=1, device_id={"col": left}, device_id_type=pl.DeviceIdType.MESH)

    @pl.when(has_right)
    def _():
        pl.semaphore_signal(barrier, inc=1, device_id={"col": right}, device_id_type=pl.DeviceIdType.MESH)

    pl.semaphore_wait(barrier, bits + has_left.astype(jnp.int32) + has_right.astype(jnp.int32))

    ready = set()

    def need(key, copy):
        if key not in ready:
            ready.add(key)
            copy.wait()

    def own_rows():
        return pl.ds(pl.multiple_of(c * hc, 16), hc)

    def gather(k):
        cur[k, :, own_rows(), :] = noise[0:rounds, k * hc : (k + 1) * hc, :].astype(BF16)

        def chunk(j, d, t, to):
            ref = cur.at[k, :, pl.ds(pl.multiple_of(j * hc, 16), hc), :]
            return remote(ref, ref, g_ss.at[k, d, t], g_rs.at[k, d, t], "col", to)

        for t in range(nc - 1):

            @pl.when(has_right & (c >= t))
            def _():
                chunk(c - t, 0, t, right).start()

            @pl.when(has_left & (c + t < nc))
            def _():
                chunk(c + t, 1, t, left).start()

            yield

            @pl.when(c - 1 - t >= 0)
            def _():
                chunk(c - 1 - t, 0, t, right).wait_recv()

            @pl.when(c + 1 + t < nc)
            def _():
                chunk(c + 1 + t, 1, t, left).wait_recv()

        for t in range(nc - 1):

            @pl.when(has_right & (c >= t))
            def _():
                chunk(c - t, 0, t, right).wait_send()

            @pl.when(has_left & (c + t < nc))
            def _():
                chunk(c + t, 1, t, left).wait_send()

    def inverse(s, k):
        need(("dv", s), dv_copy[s])
        lhs = jnp.concatenate([cur[k, d] for d in range(rounds)], axis=-1)

        @pl.loop(0, width // QB)
        def _(i):
            q = pl.ds(pl.multiple_of(i * QB, QB), QB)
            rhs = jnp.concatenate([dv[s, d, q, :] for d in range(rounds)], axis=-1)
            wsum[k, :, q] = dot_t(lhs, rhs)

    def rowsum(s, k):
        order = list(range(bits))
        if k % 2 == 1:
            order = order[:1] + order[1:][::-1]
        base = jnp.int32(0)
        size = rows
        place = 0
        for i, b in enumerate(order):
            half = size // 2
            bit = (r // (1 << b)) % 2
            keep = pl.multiple_of(base + bit * half, 16)
            away = pl.multiple_of(base + (1 - bit) * half, 16)
            area = pl.ds(place, half)
            rsend[k, area, :] = wsum[k, pl.ds(away, half), :].astype(BF16)
            copy = remote(
                rsend.at[k, area], rrecv.at[s, k, area], r_ss.at[s, k, i], r_rs.at[s, k, i], "row", partner(b)
            )
            copy.start()
            yield
            copy.wait_recv()
            total = wsum[k, pl.ds(keep, half), :] + rrecv[s, k, area, :].astype(F32)
            if i < bits - 1:
                wsum[k, pl.ds(keep, half), :] = total
            else:
                st[s, k, pl.ds(keep, half), :] = total.astype(BF16)
            copy.wait_send()
            base, size = keep, half
            place += half
        for i, b in reversed(list(enumerate(order))):
            bit = (r // (1 << b)) % 2
            mine = st.at[s, k, pl.ds(pl.multiple_of(base, 16), size)]
            j = bits + i
            copy = remote(mine, mine, r_ss.at[s, k, j], r_rs.at[s, k, j], "row", partner(b))
            copy.start()
            yield
            copy.wait()
            base = base - bit * size
            size = size * 2
        for j in range(nc):
            pltpu.make_async_copy(
                st.at[s, k, pl.ds(j * hc, hc)],
                out_solved.at[s, j, pl.ds(k * hc, hc)],
                out_sem.at[s, k, j],
            ).start()

    def colsum(s, k):
        mine = [(i, t) for i, (s_, t) in enumerate(pairs) if s_ == s]
        for i, _ in mine:
            need(("lp", i), lp_copy[i])

        @pl.loop(0, rounds)
        def _(a):
            pz[k, a] = -sum(dot_t(st[t, k], lp[i, a]) for i, t in mine)
            pz[k, a, own_rows(), :] += noise[s * rounds + a, k * hc : (k + 1) * hc, :]

        def message(a, d, to):
            return remote(
                zsend.at[k, d, a], zrecv.at[s - 1, k, d, a], z_ss.at[s - 1, k, d, a], z_rs.at[s - 1, k, d, a], "col", to
            )

        def move(a, d, receives, sends, to):
            @pl.when((a >= 0) & (a < rounds))
            def _():
                @pl.when(receives)
                def _():
                    message(a, d, to).wait_recv()

                @pl.when(sends & receives)
                def _():
                    zsend[k, d, a] = (pz[k, a] + zrecv[s - 1, k, d, a].astype(F32)).astype(BF16)

                @pl.when(sends & jnp.logical_not(receives))
                def _():
                    zsend[k, d, a] = pz[k, a].astype(BF16)

                @pl.when(sends)
                def _():
                    message(a, d, to).start()

        for tau in range(rounds + nc - 1):
            move(tau - c, 0, has_left, has_right, right)
            move(tau - (nc - 1 - c), 1, has_right, has_left, left)
            yield

        @pl.loop(0, rounds)
        def _(a):
            @pl.when(has_left)
            def _():
                pz[k, a] += zrecv[s - 1, k, 0, a].astype(F32)

            @pl.when(has_right)
            def _():
                pz[k, a] += zrecv[s - 1, k, 1, a].astype(F32)

            cur[k, a] = pz[k, a].astype(BF16)
            out_rest[s * rounds + a, k * hc : (k + 1) * hc, :] = pz[k, a, own_rows(), :]

            @pl.when(has_right)
            def _():
                message(a, 0, right).wait_send()

            @pl.when(has_left)
            def _():
                message(a, 1, left).wait_send()

    def chain(k):
        yield from gather(k)
        for s in range(steps):
            inverse(s, k)
            yield from rowsum(s, k)
            if s < steps - 1:
                yield from colsum(s + 1, k)

    live = [chain(k) for k in range(CHAINS)]
    while live:
        for one in list(live):
            if next(one, live) is live:
                live.remove(one)

    out_rest[0:rounds] = noise[0:rounds]

    def part(g, d, j, to):
        ref = frecv.at[d, g, j]
        return remote(ref, ref, f_ss.at[d, g, j], f_rs.at[d, g, j], "col", to)

    def pass_on(g, d, receives, lo, hi, to):
        @pl.when((g >= 0) & (g < groups))
        def _():
            @pl.when(receives)
            def _():
                part(g, d, c, to).wait_recv()

            def one(i, _):
                j = (hi - 1 - i) if d == 0 else (lo + i)

                @pl.when(receives)
                def _():
                    part(g, d, j, to).wait_recv()
                    frecv[d, g, j] = (pf[g, :, j] + frecv[d, g, j].astype(F32)).astype(BF16)

                @pl.when(jnp.logical_not(receives))
                def _():
                    frecv[d, g, j] = pf[g, :, j].astype(BF16)

                part(g, d, j, to).start()
                return 0

            lax.fori_loop(0, hi - lo, one, 0)

    lag = jnp.maximum(c, nc - 1 - c)

    def turn(tau, _):
        @pl.when(tau < groups)
        def _():
            for t in range(steps):
                lf_copy(tau, t).wait()
            slot = lax.rem(tau, SLOTS)
            for k in range(CHAINS):
                acc = sum(dot_t(st[t, k], lf[slot, t].reshape(gs * 128, width)) for t in range(steps))
                pf[tau, k] = -acc.reshape(nc, hc, gs * 128)

            @pl.when(tau + SLOTS < groups)
            def _():
                for t in range(steps):
                    lf_copy(tau + SLOTS, t).start()

        pass_on(tau - c, 0, has_left, c + 1, nc, right)
        pass_on(tau - (nc - 1 - c), 1, has_right, 0, c, left)
        g = tau - lag

        @pl.when((g >= 0) & (g < groups))
        def _():
            @pl.when(has_left)
            def _():
                pf[g, :, c] += frecv[0, g, c].astype(F32)

            @pl.when(has_right)
            def _():
                pf[g, :, c] += frecv[1, g, c].astype(F32)

            for i in range(gs):
                a = steps * rounds + g * gs + i
                total = pf[g, :, c, :, i * 128 : (i + 1) * 128].reshape(hl, 128)
                out_rest[a] = noise[a] + total

        return 0

    lax.fori_loop(0, groups + nc - 1, turn, 0)

    def finish(g, _):
        def sent(d, to):
            def one(j, _):
                part(g, d, j, to).wait_send()
                return 0

            return one

        lax.fori_loop(c + 1, nc, sent(0, right), 0)
        lax.fori_loop(0, c, sent(1, left), 0)
        return 0

    lax.fori_loop(0, groups, finish, 0)
    for s in range(steps):
        for k in range(CHAINS):
            for j in range(nc):
                pltpu.make_async_copy(
                    st.at[s, k, pl.ds(j * hc, hc)],
                    out_solved.at[s, j, pl.ds(k * hc, hc)],
                    out_sem.at[s, k, j],
                ).wait()


def local(nr, nc, noise, factor, dinv):
    hl, rblk, rb = noise.shape
    steps, width, rounds, _ = dinv.shape
    below = factor.shape[0] - (steps - 1) * rounds
    gs = next(x for x in (3, 2, 1) if below % x == 0)
    groups = below // gs
    hc = hl // CHAINS
    rows = nc * hc
    bits = nr.bit_length() - 1
    vm = pltpu.VMEM
    dma = pltpu.SemaphoreType.DMA
    npairs = steps * (steps - 1) // 2
    solved, rest = pl.pallas_call(
        functools.partial(kernel, nr, nc),
        out_shape=(
            jax.ShapeDtypeStruct((steps, nc, hl, width), BF16),
            jax.ShapeDtypeStruct((rblk, hl, rb), F32),
        ),
        in_specs=[
            pl.BlockSpec(memory_space=pltpu.VMEM),
            pl.BlockSpec(memory_space=pl.ANY),
            pl.BlockSpec(memory_space=pl.ANY),
        ],
        out_specs=(pl.BlockSpec(memory_space=pl.ANY), pl.BlockSpec(memory_space=pltpu.VMEM)),
        scratch_shapes=[
            vm((steps, rounds, width, rb), BF16),
            vm((npairs, rounds, rb, width), BF16),
            vm((SLOTS, steps, gs, rb, width), BF16),
            vm((steps, CHAINS, rows, width), BF16),
            vm((CHAINS, rounds, rows, rb), BF16),
            vm((CHAINS, rows, width), F32),
            vm((CHAINS, rows, width), BF16),
            vm((steps, CHAINS, rows, width), BF16),
            vm((CHAINS, rounds, rows, rb), F32),
            vm((CHAINS, 2, rounds, rows, rb), BF16),
            vm((steps - 1, CHAINS, 2, rounds, rows, rb), BF16),
            vm((groups, CHAINS, nc, hc, gs * rb), F32),
            vm((2, groups, nc, CHAINS, hc, gs * rb), BF16),
            dma((steps,)),
            dma((npairs,)),
            dma((SLOTS, steps)),
            dma((steps, CHAINS, nc)),
            dma((CHAINS, 2, nc)),
            dma((CHAINS, 2, nc)),
            dma((steps, CHAINS, 2 * bits)),
            dma((steps, CHAINS, 2 * bits)),
            dma((steps - 1, CHAINS, 2, rounds)),
            dma((steps - 1, CHAINS, 2, rounds)),
            dma((2, groups, nc)),
            dma((2, groups, nc)),
        ],
        compiler_params=pltpu.CompilerParams(
            collective_id=0, has_side_effects=True, vmem_limit_bytes=60 * 1024 * 1024
        ),
    )(
        jnp.transpose(noise, (1, 0, 2)),
        jnp.transpose(factor, (0, 2, 1, 3)),
        jnp.transpose(dinv, (0, 2, 1, 3)),
    )
    solved = jnp.transpose(solved.reshape(steps, nc * hl, width), (0, 2, 1))
    return solved, jnp.transpose(rest, (1, 0, 2))


def solution(mesh):
    placed = (P("col", None, "row"), P(None, "row", None, "col"), P(None, "col", None, "row"))
    return jax.shard_map(
        functools.partial(local, mesh.shape["row"], mesh.shape["col"]),
        mesh=mesh,
        in_specs=placed,
        out_specs=(P(None, "col", None), P("col", None, "row")),
        check_vma=False,
    )
```

time: 659 us -> 212 us (0.32)
  waiting for transfers between devices: 352 us -> 0 us
  blocking collectives: 237 us -> 0 us
  Pallas kernels: 0 us -> 203 us
  matrix products: 39.6 us -> 0 us
  between operations: 13.8 us -> 0.65 us
  other arithmetic: 10.2 us -> 0 us
    reduce_scatter x3 -> x0, waiting for transfers between devices: 352 us -> none  [local(): lax.psum_scatter(lax.dot_general(solution_wide, panel_rows, (((0,), (2,))...]
    pallas_call x0 -> x1, Pallas kernels: none -> 203 us  [local(): pl.pallas_call(functools.partial(kernel, nr, nc), out_shape=(jax.ShapeDty...]
    psum x3 -> x0, blocking collectives: 182 us -> none  [local(): solution = lax.psum(partial_sum, 'row').astype(jnp.bfloat16)]
    all_gather x3 -> x0, blocking collectives: 54.6 us -> none  [local(): lax.all_gather(current, 'col', axis=0, tiled=True).astype(jnp.float32)]
    dot_general x6 -> x0, matrix products: 39.6 us -> none  [the longest x3 28.6 us: local(): lax.dot_general(solution_wide, panel_rows, (((0,), (2,)), ((), ())))]
    scatter-add x3 -> x0, other arithmetic: 6.61 us -> none  [local(): work = work.at[:, (step_idx + 1) * rounds:, :].add(-reduced)]
  transfers between devices with their start and end apart: 3 -> 0, of which waited for: 3 -> 0; matrix products, arithmetic and copies ran while one was open for 1% -> 0% of each run, Pallas kernels for 0% -> 0%
where the time goes in v2:
time: 212 us
  Pallas kernels  203 us (96%)
  local copies, waits for them, and re-layouts  7.83 us (4%)
    pallas_call x1, Pallas kernels, local(): pl.pallas_call(functools.partial(kernel, nr, nc), out_shape=(jax.ShapeDty...  203 us
    reshape x1, local copies, waits for them, and re-layouts, local(): solved = jnp.transpose(solved.reshape(steps, nc * hl, width), (0, 2, 1))  6.42 us

profile of v2, /device:TPU:0, one launch (start us, length us, event | category | flops | bytes accessed | tf_op | source)
XLA Modules:
  0.0 211.8 jit_solution(2395616362145000541)
XLA Ops:
  0.6 203.3 %shard_map.50 = (bf16[3,4,128,1280]{3,2,1,0:T(8,128)(2,1)}, f32[36,128,128]{2,1,0:T(8,128)}) custom-call(f32[36,128,128]{2,1,0:T(8,128)} %bitcast.10, bf16[31,3,128,1280]{3,2,1,0:T(8,128)(2,1)} %bitcast.6, bf16[3,5,1280,128]{3,2,1,0:T(8,128)(2,1)} %bitcast.7), custom_call_target="tpu_custom_call" | custom-call | tf_op jit(solution)/shard_map/pallas_call | solution.py:371
  203.9 0.0 copy-start
  203.9 6.4 %copy.5 = bf16[3,512,1280]{1,2,0:T(8,128)(2,1)} copy(bf16[3,512,1280]{2,1,0:T(8,128)(2,1)} %bitcast.9) | data formatting | bytes 7864320 | tf_op jit(solution)/shard_map/reshape | solution.py:418
  210.3 0.0 copy-done
  210.3 1.4 copy.7
Async XLA Ops:
  203.9 6.4 %copy-start = (f32[36,128,128]{2,1,0:T(8,128)S(1)}, f32[36,128,128]{2,1,0:T(8,128)}, u32[]{:S(2)}) copy-start(f32[36,128,128]{2,1,0:T(8,128)} %get-tuple-element.5) | copy-start | bytes 7077892

commit v3 on v2

--- a/solution.py
+++ b/solution.py
@@ -10,7 +10,8 @@
 BF16 = jnp.bfloat16
 F32 = jnp.float32
 CHAINS = 2
-SLOTS = 3
+SLOTS = 2
+LAG = 7
 QB = 256
 
 
@@ -32,14 +33,14 @@
 def kernel(
     nr, nc, noise, factor, dinv, out_solved, out_rest,
     dv, lp, lf, st, cur, wsum, rsend, rrecv, pz, zsend, zrecv, pf, frecv,
-    dv_sem, lp_sem, lf_sem, out_sem,
+    dv_sem, lp_sem, lf_sem,
     g_ss, g_rs, r_ss, r_rs, z_ss, z_rs, f_ss, f_rs,
 ):
     steps, rounds, width = dv.shape[0], dv.shape[1], dv.shape[2]
     hl = noise.shape[1]
     hc = hl // CHAINS
     rows = nc * hc
-    groups, gs = pf.shape[0], lf.shape[2]
+    groups, gs = pf.shape[0], lf.shape[3]
     bits = nr.bit_length() - 1
     first = (steps - 1) * rounds
     r = lax.axis_index("row")
@@ -59,17 +60,18 @@
         for i, (s, t) in enumerate(pairs)
     ]
 
-    def lf_copy(group, t):
+    def lf_copy(k, group, t):
         slot = lax.rem(group, SLOTS)
         return pltpu.make_async_copy(
-            factor.at[pl.ds(first + group * gs, gs), t], lf.at[slot, t], lf_sem.at[slot, t]
+            factor.at[pl.ds(first + group * gs, gs), t], lf.at[k, slot, t], lf_sem.at[k, slot, t]
         )
 
     for copy in dv_copy + lp_copy:
         copy.start()
-    for group in range(min(SLOTS, groups)):
-        for t in range(steps):
-            lf_copy(group, t).start()
+    for k in range(CHAINS):
+        for group in range(min(SLOTS, groups)):
+            for t in range(steps):
+                lf_copy(k, jnp.int32(group), t).start()
 
     barrier = pltpu.get_barrier_semaphore()
     for b in range(bits):
@@ -182,12 +184,6 @@
             copy.wait()
             base = base - bit * size
             size = size * 2
-        for j in range(nc):
-            pltpu.make_async_copy(
-                st.at[s, k, pl.ds(j * hc, hc)],
-                out_solved.at[s, j, pl.ds(k * hc, hc)],
-                out_sem.at[s, k, j],
-            ).start()
 
     def colsum(s, k):
         mine = [(i, t) for i, (s_, t) in enumerate(pairs) if s_ == s]
@@ -249,14 +245,86 @@
             def _():
                 message(a, 1, left).wait_send()
 
+    def part(k, g, d, j, to):
+        ref = frecv.at[d, g, k, j]
+        return remote(ref, ref, f_ss.at[d, g, k, j], f_rs.at[d, g, k, j], "col", to)
+
+    def pass_on(k, g, d, receives, lo, hi, to):
+        @pl.when((g >= 0) & (g < groups))
+        def _():
+            def one(i, _):
+                j = (hi - 1 - i) if d == 0 else (lo + i)
+
+                @pl.when(receives)
+                def _():
+                    part(k, g, d, j, to).wait_recv()
+                    frecv[d, g, k, j] = (pf[g, k, j] + frecv[d, g, k, j].astype(F32)).astype(BF16)
+
+                @pl.when(jnp.logical_not(receives))
+                def _():
+                    frecv[d, g, k, j] = pf[g, k, j].astype(BF16)
+
+                part(k, g, d, j, to).start()
+                return 0
+
+            lax.fori_loop(0, hi - lo, one, 0)
+
+    lag = jnp.maximum(c, nc - 1 - c)
+
+    def turn(k, tau):
+        @pl.when(tau < groups)
+        def _():
+            for t in range(steps):
+                lf_copy(k, tau, t).wait()
+            slot = lax.rem(tau, SLOTS)
+            acc = sum(dot_t(st[t, k], lf[k, slot, t].reshape(gs * 128, width)) for t in range(steps))
+            pf[tau, k] = -acc.reshape(nc, hc, gs * 128)
+
+            @pl.when(tau + SLOTS < groups)
+            def _():
+                for t in range(steps):
+                    lf_copy(k, tau + SLOTS, t).start()
+
+        pass_on(k, tau - c, 0, has_left, c + 1, nc, right)
+        pass_on(k, tau - (nc - 1 - c), 1, has_right, 0, c, left)
+        g = tau - lag
+
+        @pl.when((g >= 0) & (g < groups))
+        def _():
+            @pl.when(has_left)
+            def _():
+                part(k, g, 0, c, right).wait_recv()
+                pf[g, k, c] += frecv[0, g, k, c].astype(F32)
+
+            @pl.when(has_right)
+            def _():
+                part(k, g, 1, c, left).wait_recv()
+                pf[g, k, c] += frecv[1, g, k, c].astype(F32)
+
+            for i in range(gs):
+                a = steps * rounds + g * gs + i
+                total = pf[g, k, c, :, i * 128 : (i + 1) * 128]
+                out_rest[a, k * hc : (k + 1) * hc, :] = noise[a, k * hc : (k + 1) * hc, :] + total
+
+    turns = groups + nc - 1
+    taken = [0] * CHAINS
+
     def chain(k):
+        for _ in range(k * LAG):
+            yield
         yield from gather(k)
         for s in range(steps):
             inverse(s, k)
             yield from rowsum(s, k)
             if s < steps - 1:
                 yield from colsum(s + 1, k)
-
+        over.add(k)
+        while len(over) < CHAINS and taken[k] < turns:
+            turn(k, jnp.int32(taken[k]))
+            taken[k] += 1
+            yield
+
+    over = set()
     live = [chain(k) for k in range(CHAINS)]
     while live:
         for one in list(live):
@@ -264,96 +332,47 @@
                 live.remove(one)
 
     out_rest[0:rounds] = noise[0:rounds]
-
-    def part(g, d, j, to):
-        ref = frecv.at[d, g, j]
-        return remote(ref, ref, f_ss.at[d, g, j], f_rs.at[d, g, j], "col", to)
-
-    def pass_on(g, d, receives, lo, hi, to):
-        @pl.when((g >= 0) & (g < groups))
+    owners = max(1, 128 // hl)
+    units = steps * (nc // owners)
+    count = turns - min(taken)
+    per = -(-units // count)
+
+    def turn_over(u):
+        @pl.when(u < units)
         def _():
-            @pl.when(receives)
-            def _():
-                part(g, d, c, to).wait_recv()
-
-            def one(i, _):
-                j = (hi - 1 - i) if d == 0 else (lo + i)
-
-                @pl.when(receives)
-                def _():
-                    part(g, d, j, to).wait_recv()
-                    frecv[d, g, j] = (pf[g, :, j] + frecv[d, g, j].astype(F32)).astype(BF16)
-
-                @pl.when(jnp.logical_not(receives))
-                def _():
-                    frecv[d, g, j] = pf[g, :, j].astype(BF16)
-
-                part(g, d, j, to).start()
+            s = u // (nc // owners)
+            v = u % (nc // owners)
+            blocks = [
+                st[s, k, pl.ds(pl.multiple_of((v * owners + o) * hc, 16), hc), :]
+                for o in range(owners)
+                for k in range(CHAINS)
+            ]
+            tile = jnp.concatenate(blocks, axis=0).astype(F32)
+            out_solved[s, :, pl.ds(pl.multiple_of(v * 128, 128), 128)] = tile.T.astype(BF16)
+
+    def both(i, _):
+        for k in range(CHAINS):
+            turn(k, taken[k] + i)
+        for p in range(per):
+            turn_over(i * per + p)
+        return 0
+
+    lax.fori_loop(0, count, both, 0)
+
+    def finish(g, _):
+        def sent(k, d, to):
+            def one(j, _):
+                part(k, g, d, j, to).wait_send()
                 return 0
 
-            lax.fori_loop(0, hi - lo, one, 0)
-
-    lag = jnp.maximum(c, nc - 1 - c)
-
-    def turn(tau, _):
-        @pl.when(tau < groups)
-        def _():
-            for t in range(steps):
-                lf_copy(tau, t).wait()
-            slot = lax.rem(tau, SLOTS)
-            for k in range(CHAINS):
-                acc = sum(dot_t(st[t, k], lf[slot, t].reshape(gs * 128, width)) for t in range(steps))
-                pf[tau, k] = -acc.reshape(nc, hc, gs * 128)
-
-            @pl.when(tau + SLOTS < groups)
-            def _():
-                for t in range(steps):
-                    lf_copy(tau + SLOTS, t).start()
-
-        pass_on(tau - c, 0, has_left, c + 1, nc, right)
-        pass_on(tau - (nc - 1 - c), 1, has_right, 0, c, left)
-        g = tau - lag
-
-        @pl.when((g >= 0) & (g < groups))
-        def _():
-            @pl.when(has_left)
-            def _():
-                pf[g, :, c] += frecv[0, g, c].astype(F32)
-
-            @pl.when(has_right)
-            def _():
-                pf[g, :, c] += frecv[1, g, c].astype(F32)
-
-            for i in range(gs):
-                a = steps * rounds + g * gs + i
-                total = pf[g, :, c, :, i * 128 : (i + 1) * 128].reshape(hl, 128)
-                out_rest[a] = noise[a] + total
-
+            return one
+
+        for k in range(CHAINS):
+            lax.fori_loop(c + 1, nc, sent(k, 0, right), 0)
+            lax.fori_loop(0, c, sent(k, 1, left), 0)
         return 0
 
-    lax.fori_loop(0, groups + nc - 1, turn, 0)
-
-    def finish(g, _):
-        def sent(d, to):
-            def one(j, _):
-                part(g, d, j, to).wait_send()
-                return 0
-
-            return one
-
-        lax.fori_loop(c + 1, nc, sent(0, right), 0)
-        lax.fori_loop(0, c, sent(1, left), 0)
-        return 0
-
     lax.fori_loop(0, groups, finish, 0)
-    for s in range(steps):
-        for k in range(CHAINS):
-            for j in range(nc):
-                pltpu.make_async_copy(
-                    st.at[s, k, pl.ds(j * hc, hc)],
-                    out_solved.at[s, j, pl.ds(k * hc, hc)],
-                    out_sem.at[s, k, j],
-                ).wait()
 
 
 def local(nr, nc, noise, factor, dinv):
@@ -371,7 +390,7 @@
     solved, rest = pl.pallas_call(
         functools.partial(kernel, nr, nc),
         out_shape=(
-            jax.ShapeDtypeStruct((steps, nc, hl, width), BF16),
+            jax.ShapeDtypeStruct((steps, width, nc * hl), BF16),
             jax.ShapeDtypeStruct((rblk, hl, rb), F32),
         ),
         in_specs=[
@@ -379,11 +398,11 @@
             pl.BlockSpec(memory_space=pl.ANY),
             pl.BlockSpec(memory_space=pl.ANY),
         ],
-        out_specs=(pl.BlockSpec(memory_space=pl.ANY), pl.BlockSpec(memory_space=pltpu.VMEM)),
+        out_specs=(pl.BlockSpec(memory_space=pltpu.VMEM), pl.BlockSpec(memory_space=pltpu.VMEM)),
         scratch_shapes=[
             vm((steps, rounds, width, rb), BF16),
             vm((npairs, rounds, rb, width), BF16),
-            vm((SLOTS, steps, gs, rb, width), BF16),
+            vm((CHAINS, SLOTS, steps, gs, rb, width), BF16),
             vm((steps, CHAINS, rows, width), BF16),
             vm((CHAINS, rounds, rows, rb), BF16),
             vm((CHAINS, rows, width), F32),
@@ -393,29 +412,27 @@
             vm((CHAINS, 2, rounds, rows, rb), BF16),
             vm((steps - 1, CHAINS, 2, rounds, rows, rb), BF16),
             vm((groups, CHAINS, nc, hc, gs * rb), F32),
-            vm((2, groups, nc, CHAINS, hc, gs * rb), BF16),
+            vm((2, groups, CHAINS, nc, hc, gs * rb), BF16),
             dma((steps,)),
             dma((npairs,)),
-            dma((SLOTS, steps)),
-            dma((steps, CHAINS, nc)),
+            dma((CHAINS, SLOTS, steps)),
             dma((CHAINS, 2, nc)),
             dma((CHAINS, 2, nc)),
             dma((steps, CHAINS, 2 * bits)),
             dma((steps, CHAINS, 2 * bits)),
             dma((steps - 1, CHAINS, 2, rounds)),
             dma((steps - 1, CHAINS, 2, rounds)),
-            dma((2, groups, nc)),
-            dma((2, groups, nc)),
+            dma((2, groups, CHAINS, nc)),
+            dma((2, groups, CHAINS, nc)),
         ],
         compiler_params=pltpu.CompilerParams(
-            collective_id=0, has_side_effects=True, vmem_limit_bytes=60 * 1024 * 1024
+            collective_id=0, has_side_effects=True, vmem_limit_bytes=63 * 1024 * 1024
         ),
     )(
         jnp.transpose(noise, (1, 0, 2)),
         jnp.transpose(factor, (0, 2, 1, 3)),
         jnp.transpose(dinv, (0, 2, 1, 3)),
     )
-    solved = jnp.transpose(solved.reshape(steps, nc * hl, width), (0, 2, 1))
     return solved, jnp.transpose(rest, (1, 0, 2))
 
 

time: 212 us -> 211 us (level)
    reshape x1 -> x0, local copies, waits for them, and re-layouts: 6.42 us -> none  [local(): solved = jnp.transpose(solved.reshape(steps, nc * hl, width), (0, 2, 1))]
    unnamed x3 -> x4, local copies, waits for them, and re-layouts: 1.41 us -> 5.85 us
where the time goes in v3:
time: 211 us
  Pallas kernels  205 us (97%)
  local copies, waits for them, and re-layouts  5.85 us (3%)
    pallas_call x1, Pallas kernels, local(): pl.pallas_call(functools.partial(kernel, nr, nc), out_shape=(jax.ShapeDty...  205 us
    unnamed x4, local copies, waits for them, and re-layouts  5.85 us

profile of v3, /device:TPU:0, one launch (start us, length us, event | category | flops | bytes accessed | tf_op | source)
XLA Modules:
  0.0 211.2 jit_solution(14641326470904825813)
XLA Ops:
  0.6 204.7 %shard_map.50 = (bf16[3,1280,512]{2,1,0:T(8,128)(2,1)}, f32[36,128,128]{2,1,0:T(8,128)}) custom-call(f32[36,128,128]{2,1,0:T(8,128)} %bitcast.6, bf16[31,3,128,1280]{3,2,1,0:T(8,128)(2,1)} %bitcast.4, bf16[3,5,1280,128]{3,2,1,0:T(8,128)(2,1)} %bitcast.5), custom_call_target="tpu_custom_call" | custom-call | tf_op jit(solution)/shard_map/pallas_call | solution.py:390
  205.3 0.0 copy-start
  205.3 4.4 %copy.7 = bf16[3,1280,512]{2,1,0:T(8,128)(2,1)} copy(bf16[3,1280,512]{2,1,0:T(8,128)(2,1)} %get-tuple-element.8) | data formatting | bytes 7864320
  209.7 0.0 copy-done
  209.7 1.4 copy.8
Async XLA Ops:
  205.3 4.5 %copy-start = (f32[36,128,128]{2,1,0:T(8,128)S(1)}, f32[36,128,128]{2,1,0:T(8,128)}, u32[]{:S(2)}) copy-start(f32[36,128,128]{2,1,0:T(8,128)} %get-tuple-element.5) | copy-start | bytes 7077892

commit v4 on v3

--- a/solution.py
+++ b/solution.py
@@ -11,7 +11,7 @@
 F32 = jnp.float32
 CHAINS = 2
 SLOTS = 2
-LAG = 7
+LAG = 0
 QB = 256
 
 
@@ -190,9 +190,12 @@
         for i, _ in mine:
             need(("lp", i), lp_copy[i])
 
+        update = sum(dot_t(st[t, k], lp[i].reshape(rounds * 128, width)) for i, t in mine)
+        for a in range(rounds):
+            pz[k, a] = -update[:, a * 128 : (a + 1) * 128]
+
         @pl.loop(0, rounds)
         def _(a):
-            pz[k, a] = -sum(dot_t(st[t, k], lp[i, a]) for i, t in mine)
             pz[k, a, own_rows(), :] += noise[s * rounds + a, k * hc : (k + 1) * hc, :]
 
         def message(a, d, to):

time: 211 us -> 203 us (0.962)
  Pallas kernels: 205 us -> 197 us
    pallas_call x1, Pallas kernels: 205 us -> 197 us  [local(): pl.pallas_call(functools.partial(kernel, nr, nc), out_shape=(jax.ShapeDty...]
where the time goes in v4:
time: 203 us
  Pallas kernels  197 us (97%)
  local copies, waits for them, and re-layouts  5.85 us (3%)
    pallas_call x1, Pallas kernels, local(): pl.pallas_call(functools.partial(kernel, nr, nc), out_shape=(jax.ShapeDty...  197 us
    unnamed x4, local copies, waits for them, and re-layouts  5.85 us

profile of v4, /device:TPU:0, one launch (start us, length us, event | category | flops | bytes accessed | tf_op | source)
XLA Modules:
  0.0 203.3 jit_solution(12094650314064524717)
XLA Ops:
  0.6 196.8 %shard_map.50 = (bf16[3,1280,512]{2,1,0:T(8,128)(2,1)}, f32[36,128,128]{2,1,0:T(8,128)}) custom-call(f32[36,128,128]{2,1,0:T(8,128)} %bitcast.6, bf16[31,3,128,1280]{3,2,1,0:T(8,128)(2,1)} %bitcast.4, bf16[3,5,1280,128]{3,2,1,0:T(8,128)(2,1)} %bitcast.5), custom_call_target="tpu_custom_call" | custom-call | tf_op jit(solution)/shard_map/pallas_call | solution.py:393
  197.4 0.0 copy-start
  197.5 4.4 %copy.7 = bf16[3,1280,512]{2,1,0:T(8,128)(2,1)} copy(bf16[3,1280,512]{2,1,0:T(8,128)(2,1)} %get-tuple-element.8) | data formatting | bytes 7864320
  201.9 0.0 copy-done
  201.9 1.4 copy.8
Async XLA Ops:
  197.4 4.5 %copy-start = (f32[36,128,128]{2,1,0:T(8,128)S(1)}, f32[36,128,128]{2,1,0:T(8,128)}, u32[]{:S(2)}) copy-start(f32[36,128,128]{2,1,0:T(8,128)} %get-tuple-element.5) | copy-start | bytes 7077892
